TPU v7x, 32 devices: a whole 2x2x4 slice. The times are simulated.
32 devices in a mesh: gx: 4 (over z), gy: 8 (over y, x, core).
Axes of the slice: x: 2, y: 2, z: 4, core: 2. Of those that a mesh axis runs over, the one named last changes fastest.
Arguments:
- velocity: float32 [3, 32, 64, 128], P(None, 'gx', 'gy'), may hold values from -1 to 1
- wall_cells: int32 [32, 64, 128], P('gx', 'gy'), may hold values 0 or 1
- tile_counts: int32 [4, 8, 8], P('gx', 'gy'), may hold values from 32 to 256, as said below
- helper_tile: int32 [4, 8], P('gx'), may hold values from 0 to 63, as said below
- base_fields: float32 [4, 8, 8, 3, 32, 1024], P('gx', 'gy'), may hold values from -2.5 to 2.5
- extra_fields: float32 [4, 8, 3, 224, 1024], P('gx', 'gy'), may hold values from -6.1 to 6.1
- base_noise: bfloat16 [4, 8, 8, 2, 3, 32, 1024], P('gx', 'gy'), may hold values from -2.5 to 2.5
- extra_noise: bfloat16 [4, 8, 2, 3, 224, 1024], P('gx', 'gy'), may hold values from -2.5 to 2.5
Outputs:
- new_base_fields: float32 [4, 8, 8, 3, 32, 1024], P('gx', 'gy')
- new_extra_fields: float32 [4, 8, 3, 224, 1024], P('gx', 'gy')
- polymer_stress: float32 [4, 8, 8, 6, 1024], P('gx', 'gy')
Inputs may be any that keep to these rules, and one draw needn't show every extreme that they name: `tile_counts`: each entry is 32 or 256. In each row of tiles exactly 8 tiles have 256, these are the tiles that helper_tile names, one column of tiles holds at most 4 of them and in every row some column holds exactly 4. `helper_tile`: entry [i, h] = o * 8 + t names tile t of column o in row i; the entries of a row are distinct and name exactly the row's tiles with 256 fields.
All inputs are finite; a program needn't handle non-finite values. No bound on the sum of `wall_cells` on one device may be relied on, other than what follows from the above.
Results may differ from a plain program's by a relative error of at most 0.0003.
Values sent between devices are 32-bit elements; how exact they have to be, the bound alone decides.
No kernel may reach another device: no remote copies, remote signals or barrier semaphores. Data moves between devices by JAX's collectives and lax.ppermute only.
A program may use at most 128 MiB of HBM per device.

v0:
```python
import functools

import jax
import jax.numpy as jnp
from jax import lax
from jax.experimental import pallas as pl
from jax.experimental.pallas import tpu as pltpu
from jax.sharding import PartitionSpec as P

ALL_FIELDS = 256
HEAVY_MOST = 4
LANES = 128
SUB = 8
SMALL = 12 << 20

time_step = 0.05
weissenberg = 0.25
max_extension = 50.0
noise_scale = (time_step / weissenberg) ** 0.5
component_pairs = ((0, 0), (1, 1), (2, 2), (0, 1), (0, 2), (1, 2))
moment_of = {(0, 0): 0, (1, 1): 1, (2, 2): 2, (0, 1): 3, (1, 0): 3, (0, 2): 4, (2, 0): 4, (1, 2): 5, (2, 1): 5}
f32 = jnp.float32

vmem = pl.BlockSpec(memory_space=pltpu.VMEM)
hbm = pl.BlockSpec(memory_space=pltpu.HBM)
anywhere = pl.BlockSpec(memory_space=pl.ANY)


def far_memory(*arrays):
    return [pltpu.with_memory_space_constraint(array, pltpu.HBM) for array in arrays]


def near_memory(*arrays):
    return [pltpu.with_memory_space_constraint(array, pltpu.VMEM) for array in arrays]


def column_sum(value):
    return jnp.sum(value, axis=0, keepdims=True)


def interleaved(a, b, bit):
    low = (lax.broadcasted_iota(jnp.int32, (SUB, LANES), 0) & bit) == 0
    return jnp.where(low, a, b) + pltpu.roll(jnp.where(low, b, a), bit, 0)


def packed_sums(values_of, count):
    stack = []
    for x in range(count):
        bit, values = 1, values_of(x)
        while stack and stack[-1][0] == bit:
            values = [interleaved(a, b, bit) for a, b in zip(stack.pop()[1], values)]
            bit *= 2
        stack.append((bit, values))
    return stack[0][1]


def wide(row):
    return jnp.broadcast_to(row, (SUB, LANES))


def turned(value, cell_z):
    sub = lax.broadcasted_iota(jnp.int32, value.shape, 0)
    group = lax.broadcasted_iota(jnp.int32, value.shape, 1) // cell_z
    skewed = pltpu.roll(value, cell_z, 1, stride=cell_z, stride_axis=0)
    mixed = jnp.take_along_axis(skewed, (group + sub) & (SUB - 1), axis=0, mode="promise_in_bounds")
    return pltpu.roll(mixed, 0, 1, stride=cell_z, stride_axis=0)


def relax_of(total, inverse):
    factor = 1.0 / (1.0 - total * inverse / max_extension)
    return 1.0 - (time_step * 0.5 / weissenberg) * factor


def stepped(vectors, noise, matrix):
    return [
        matrix[3 * a] * vectors[0]
        + matrix[3 * a + 1] * vectors[1]
        + matrix[3 * a + 2] * vectors[2]
        + noise_scale * noise[a]
        for a in range(3)
    ]


def with_diagonal(grad, relax):
    return [g + relax if i % 4 == 0 else g for i, g in enumerate(grad)]


def noise_rows(ref, start):
    both = [ref(a, pl.ds(start, 2 * SUB)).astype(f32) for a in range(3)]
    return [[w[:SUB] for w in both], [w[SUB:] for w in both]]


def add_moments(sums, q):
    return [s + q[a] * q[b] for s, (a, b) in zip(sums, component_pairs)]


def product_sums(sums, q, w):
    terms = [q[a] * q[b] for a, b in component_pairs]
    terms += [q[a] * w[b] for a in range(3) for b in range(3)]
    terms += [w[0] * w[0] + w[1] * w[1] + w[2] * w[2]]
    return [s + t for s, t in zip(sums, terms)]


def coefficients(g, m):
    cross = lambda a, b: m[6 + 3 * a + b]
    square = lambda a, b: m[moment_of[a, b]]
    once, twice, kick = 0.0, 0.0, 0.0
    for a in range(3):
        for b in range(3):
            once += g[3 * a + b] * square(a, b)
            kick += g[3 * a + b] * cross(b, a)
            inner = 0.0
            for c in range(3):
                inner += g[3 * a + c] * square(b, c)
            twice += g[3 * a + b] * inner
    return [
        twice + (2 * noise_scale) * kick + noise_scale**2 * m[15],
        2.0 * once + (2 * noise_scale) * (cross(0, 0) + cross(1, 1) + cross(2, 2)),
        m[0] + m[1] + m[2],
    ]


def owned_slots(tiles, me, helper):
    found = []
    row = helper[...]
    for h in range(helper.shape[1]):
        tile = row[0, h] - me * tiles
        found.append((h, (tile >= 0) & (tile < tiles), tile))
    return found


def owned_order(tiles, me, helper, parities=(0, 1)):
    places = jnp.int32(0)
    order = [jnp.int32(0)] * HEAVY_MOST
    for h, owned, tile in owned_slots(tiles, me, helper):
        if len(parities) == 1:
            owned = owned & (((me ^ h) & 1) == parities[0])
        entry = h * tiles + tile
        order = [jnp.where(owned & (places == k), entry, kept) for k, kept in enumerate(order)]
        places = places + owned.astype(jnp.int32)
    return places, [(entry // tiles, entry % tiles) for entry in order]


def small(flops, traffic):
    return pl.CostEstimate(flops=flops, bytes_accessed=traffic, transcendentals=0)


def is_even(axis):
    return (lax.axis_index(axis) & 1) == 0


def edges(helper, velocity, helper_near, x_one, x_two, y_one, y_two):
    depth, width = velocity.shape[1:3]
    helper_near[...] = helper[...]
    even = is_even("gx")
    for a in range(3):
        first, last = velocity[a, 0], velocity[a, depth - 1]
        x_one[a] = jnp.where(even, last, first)
        x_two[a] = jnp.where(even, first, last)
    even = is_even("gy")
    for a in range(3):
        for x in range(depth):
            first, last = velocity[a, x, pl.ds(0, 1), :], velocity[a, x, pl.ds(width - 1, 1), :]
            y_one[a, pl.ds(x, 1), :] = jnp.where(even, last, first)
            y_two[a, pl.ds(x, 1), :] = jnp.where(even, first, last)


def call_edges(helper_tile, velocity):
    _, depth, width, length = velocity.shape
    along_x = jax.ShapeDtypeStruct((3, width, length), f32)
    along_y = jax.ShapeDtypeStruct((3, depth, length), f32)
    return pl.pallas_call(
        edges,
        out_shape=(jax.ShapeDtypeStruct(helper_tile.shape, jnp.int32), along_x, along_x, along_y, along_y),
        in_specs=[vmem, vmem],
        out_specs=(vmem,) * 5,
        compiler_params=pltpu.CompilerParams(vmem_limit_bytes=4 << 20),
        cost_estimate=small(1 << 10, 1 << 17),
        name="edges",
    )(*far_memory(helper_tile, velocity))


def swap_within(block, axis):
    return lax.ppermute(block, axis, [(i, i ^ 1) for i in range(lax.axis_size(axis))])


def swap_across(block, along_rows):
    rows, columns = lax.axis_size("gx"), lax.axis_size("gy")
    size = rows if along_rows else columns

    def partner(row, column):
        place = row if along_rows else column
        if place in (0, size - 1):
            row, column = (row, column ^ 1) if along_rows else (row ^ 1, column)
        else:
            place += 1 if place & 1 else -1
            row, column = (place, column) if along_rows else (row, place)
        return row * columns + column

    places = [(row, column) for row in range(rows) for column in range(columns)]
    return lax.ppermute(block, ("gx", "gy"), [(i, partner(*place)) for i, place in enumerate(places)])


def low_and_high(axis, one, two, a):
    even, place = is_even(axis), lax.axis_index(axis)
    low = jnp.where(even, two[a], one[a])
    high = jnp.where(even, one[a], two[a])
    return jnp.where(place == 0, 0.0, low), jnp.where(place == lax.axis_size(axis) - 1, 0.0, high)


def heavy_moments(helper, base, noise, out, fields, shocks, sems):
    _, _, count, cells = fields.shape
    tiles = base.shape[2]
    me = lax.axis_index("gy")

    def loads(k, tile):
        return (
            pltpu.make_async_copy(base.at[0, 0, tile], fields.at[k], sems.at[0, k]),
            pltpu.make_async_copy(noise.at[0, 0, tile, 0], shocks.at[k], sems.at[1, k]),
        )

    places, order = owned_order(tiles, me, helper)
    for k, (_, tile) in enumerate(order):

        @pl.when(k < places)
        def _(k=k, tile=tile):
            for copy in loads(k, tile):
                copy.start()

    for k, (h, tile) in enumerate(order):

        @pl.when(k < places)
        def _(k=k, h=h, tile=tile):
            for copy in loads(k, tile):
                copy.wait()

            def sums_of(x):
                lanes = pl.ds(x * LANES, LANES)
                sums = [jnp.zeros((SUB, LANES), f32)] * 16
                for group in range(count // (2 * SUB)):
                    pair = noise_rows(lambda a, rows: shocks[k, a, rows, lanes], group * 2 * SUB)
                    for half in range(2):
                        rows = pl.ds((2 * group + half) * SUB, SUB)
                        sums = product_sums(sums, [fields[k, a, rows, lanes] for a in range(3)], pair[half])
                return sums

            for i, value in enumerate(packed_sums(sums_of, cells // LANES)):
                out[h, i] = value


def call_heavy_moments(helper_tile, base_fields, base_noise):
    slots = helper_tile.shape[1]
    count, cells = base_fields.shape[-2:]
    return pl.pallas_call(
        heavy_moments,
        out_shape=jax.ShapeDtypeStruct((slots, 16, cells // LANES, LANES), f32),
        in_specs=[vmem, hbm, hbm],
        out_specs=vmem,
        scratch_shapes=[
            pltpu.VMEM((HEAVY_MOST, 3, count, cells), f32),
            pltpu.VMEM((HEAVY_MOST, 3, count, cells), jnp.bfloat16),
            pltpu.SemaphoreType.DMA((2, HEAVY_MOST)),
        ],
        compiler_params=pltpu.CompilerParams(vmem_limit_bytes=SMALL),
        cost_estimate=small(8 << 20, 3 << 20),
        name="heavy_moments",
    )(helper_tile, *far_memory(base_fields, base_noise))


def outer_sums(sums, left, right):
    return [s + left[a] * right[b] for s, (a, b) in zip(sums, [(a, b) for a in range(3) for b in range(3)])]


def extra_moments(steps, unroll, before, base, noise, out, partial):
    _, _, _, count, cells = base.shape
    many = out.shape[0]

    @pl.loop(0, cells // LANES)
    def _(x):
        lanes = pl.ds(pl.multiple_of(x * LANES, LANES), LANES)

        def body(i, sums):
            start = pl.multiple_of(i * 2 * SUB, 2 * SUB)
            pairs = [noise_rows(lambda a, rows: noise[0, 0, step, a, rows, lanes], start) for step in range(steps)]
            for half in range(2):
                q = [base[0, 0, a, pl.ds(start + half * SUB, SUB), lanes] for a in range(3)]
                w = [pair[half] for pair in pairs]
                if steps == 1:
                    sums = add_moments(sums[:6], q) + outer_sums(sums[6:15], q, w[0]) + add_moments(sums[15:], w[0])
                else:
                    sums = outer_sums(sums[:9], q, w[1]) + outer_sums(sums[9:18], *w) + add_moments(sums[18:], w[1])
            return sums

        zero = jnp.zeros((SUB, LANES), f32)
        for i, s in enumerate(lax.fori_loop(0, count // (2 * SUB), body, [zero] * many, unroll=unroll)):
            partial[i, x] = s

    for i in range(many):
        out[i] = packed_sums(lambda x: [partial[i, x]], cells // LANES)[0]


def call_extra_moments(steps, before, extra_fields, extra_noise):
    cells = extra_fields.shape[-1]
    many = 21 if steps == 1 else 24
    return pl.pallas_call(
        functools.partial(extra_moments, steps, 7),
        out_shape=jax.ShapeDtypeStruct((many, cells // LANES, LANES), f32),
        in_specs=[anywhere, vmem, vmem],
        out_specs=vmem,
        scratch_shapes=[pltpu.VMEM((many, cells // LANES, SUB, LANES), f32)],
        compiler_params=pltpu.CompilerParams(vmem_limit_bytes=SMALL),
        cost_estimate=small(8 << 20, 5 << 20),
        name="extra_moments",
    )(before, *near_memory(extra_fields, extra_noise))


def gradients(tiles, before, helper, velocity, y_two, x_two, x_one, y_one, wall, moments, grad, keep, send):
    me = lax.axis_index("gy")
    depth = velocity.shape[1]
    cell_z = velocity.shape[3] // tiles
    sub = lax.broadcasted_iota(jnp.int32, (SUB, LANES), 0)
    lane = lax.broadcasted_iota(jnp.int32, (SUB, LANES), 1)
    z = lane % cell_z
    scales = [turned(jnp.where(wall[x] == 0, 0.5 * time_step, 0.0).astype(f32), cell_z) for x in range(depth)]
    for a in range(3):
        x_low, x_high = low_and_high("gx", x_one, x_two, a)
        y_low, y_high = low_and_high("gy", y_one, y_two, a)
        rows = [x_low] + [velocity[a, x] for x in range(depth)] + [x_high]
        rows = [turned(row, cell_z) for row in rows]
        low, high = turned(y_low, cell_z), turned(y_high, cell_z)
        for x in range(depth):
            here = rows[x + 1]
            above = high if x == depth - 1 else pltpu.roll(high, LANES - cell_z * (x + 1), 1)
            below = low if x == 0 else pltpu.roll(low, LANES - cell_z * x, 1)
            y_up = jnp.where(lane < LANES - cell_z, pltpu.roll(here, LANES - cell_z, 1), above)
            y_down = jnp.where(lane >= cell_z, pltpu.roll(here, cell_z, 1), below)
            next_tile = pltpu.roll(pltpu.roll(here, cell_z - 1, 1), 1, 0)
            last_tile = pltpu.roll(pltpu.roll(here, LANES - cell_z + 1, 1), SUB - 1, 0)
            next_tile = jnp.where(sub == 0, 0.0, next_tile)
            last_tile = jnp.where(sub == SUB - 1, 0.0, last_tile)
            z_up = jnp.where(z == cell_z - 1, next_tile, pltpu.roll(here, LANES - 1, 1))
            z_down = jnp.where(z == 0, last_tile, pltpu.roll(here, 1, 1))
            for b, difference in enumerate((rows[x + 2] - rows[x], y_up - y_down, z_up - z_down)):
                grad[pl.ds(((3 * a + b) * depth + x) * SUB, SUB), :] = difference * scales[x]
    keep[...] = jnp.zeros(keep.shape, f32)
    send[...] = jnp.zeros(send.shape, f32)
    for h, owned, tile in owned_slots(tiles, me, helper):

        @pl.when(owned)
        def _(h=h, tile=tile):
            g = [grad[pl.ds(i * depth * SUB + SUB - 1 - tile, depth, stride=SUB), :] for i in range(9)]
            rows = g + coefficients(g, [moments[h, i] for i in range(16)])
            stays = (me & 1) == (h & 1)

            @pl.when(stays)
            def _():
                for i, row in enumerate(rows):
                    keep[h >> 1, i] = row

            @pl.when(jnp.logical_not(stays))
            def _():
                for i, row in enumerate(rows):
                    send[h >> 1, i] = row


def call_gradients(tiles, before, helper_tile, velocity, halos, wall_cells, moments):
    slots = helper_tile.shape[1]
    depth = velocity.shape[1]
    half = jax.ShapeDtypeStruct((slots // 2, 12, depth, LANES), f32)
    return pl.pallas_call(
        functools.partial(gradients, tiles),
        out_shape=(jax.ShapeDtypeStruct((9 * depth * SUB, LANES), f32), half, half),
        in_specs=[anywhere] + [vmem] * 8,
        out_specs=(vmem,) * 3,
        compiler_params=pltpu.CompilerParams(vmem_limit_bytes=8 << 20),
        cost_estimate=small(4 << 20, 1 << 20),
        name="gradients",
    )(before, helper_tile, velocity, *halos, wall_cells, moments)


def swapped(block, flip):
    size = lax.axis_size("gy")
    return lax.ppermute(block, "gy", [(i, i ^ flip) for i in range(size)])


def merge(before, kept, received, keep, *sends):
    pair = lax.axis_index("gy") >> 1
    for flip, out in enumerate((keep,) + sends):
        out[...] = kept[pair ^ flip] + received[pair ^ flip]


def call_merge(before, kept, received):
    one = jax.ShapeDtypeStruct(kept.shape[1:], f32)
    return pl.pallas_call(
        merge,
        out_shape=(one,) * kept.shape[0],
        in_specs=[anywhere, vmem, vmem],
        out_specs=(vmem,) * kept.shape[0],
        compiler_params=pltpu.CompilerParams(vmem_limit_bytes=4 << 20),
        cost_estimate=small(1 << 10, 1 << 18),
        name="merge",
    )(before, kept, received)


def join(before, *refs):
    for i, ref in enumerate(refs[:-1]):
        refs[-1][i] = ref[...]


def call_join(before, blocks):
    return pl.pallas_call(
        join,
        out_shape=jax.ShapeDtypeStruct((len(blocks),) + blocks[0].shape, f32),
        in_specs=[anywhere] + [vmem] * len(blocks),
        out_specs=vmem,
        compiler_params=pltpu.CompilerParams(vmem_limit_bytes=4 << 20),
        cost_estimate=small(1 << 10, 1 << 18),
        name="join",
    )(before, *blocks)


def stress_rows(sums, inverse):
    second = [s * inverse for s in sums]
    stretch = 1.0 / (1.0 - (second[0] + second[1] + second[2]) / max_extension)
    return [(stretch * s - (1.0 if i < 3 else 0.0)) * (1.0 / weissenberg) for i, s in enumerate(second)]


def tile_grad(grad, depth, tile, x):
    return [wide(grad[pl.ds((i * depth + x + 1) * SUB - 1 - tile, 1), :]) for i in range(9)]


def tile_sums(read, write, noise, matrices, count, add, many):
    sums = [jnp.zeros((SUB, LANES), f32)] * many
    for group in range(count // (2 * SUB)):
        pairs = [noise_rows(functools.partial(noise, step), group * 2 * SUB) for step in range(len(matrices))]
        for half in range(2):
            rows = pl.ds((2 * group + half) * SUB, SUB)
            q = [read(a, rows) for a in range(3)]
            for step, matrix in enumerate(matrices):
                q = stepped(q, pairs[step][half], matrix)
            for a in range(3):
                write(a, rows, q[a])
            sums = add(sums, q)
    return sums


def add_square(sums, q):
    return [sums[0] + (q[0] * q[0] + q[1] * q[1] + q[2] * q[2])]


def ordinary(first, direct, has_block, has_base, has_extra, *refs):
    refs = list(refs)
    before, base, noise, grad = refs[:4]
    del refs[:4]
    block = refs.pop(0) if has_block else None
    if has_base:
        refs.pop(0)
    extra, extra_noise, drive = [refs.pop(0) for _ in range(3)] if has_extra else [None] * 3
    new_base = refs.pop(0) if has_block or direct else None
    new_extra = refs.pop(0) if has_extra else None
    fields, stress, early, halfway, relaxes, advanced, sems = refs
    _, _, count, cells = fields.shape
    here = direct + fields.shape[0]
    depth = cells // LANES
    inverse = 1.0 / count
    copies = []
    if has_block:
        last = block.shape[0]
        copies += [
            pltpu.make_async_copy(block.at[i], new_base.at[0, 0, first - last + i], sems.at[i]) for i in range(last)
        ]
    for copy in copies:
        copy.start()
    if has_extra:
        at = len(copies)

        def leave(x):
            lanes = pl.ds(x * LANES, LANES)
            return pltpu.make_async_copy(advanced.at[:, :, lanes], new_extra.at[0, 0, :, :, lanes], sems.at[at + x])

        @pl.loop(0, depth)
        def _(x):
            lanes = pl.ds(pl.multiple_of(x * LANES, LANES), LANES)
            rows_of = [wide(drive[i, pl.ds(x, 1), :]) for i in range(11)]
            matrices = [with_diagonal(rows_of[:9], rows_of[9 + step]) for step in range(2)]

            def body(i, carry):
                start = pl.multiple_of(i * 2 * SUB, 2 * SUB)
                pairs = [
                    noise_rows(lambda a, rows: extra_noise[0, 0, step, a, rows, lanes], start) for step in range(2)
                ]
                for half in range(2):
                    rows = pl.ds(start + half * SUB, SUB)
                    q = [extra[0, 0, a, rows, lanes] for a in range(3)]
                    for step in range(2):
                        q = stepped(q, pairs[step][half], matrices[step])
                    for a in range(3):
                        advanced[a, rows, lanes] = q[a]
                return carry

            lax.fori_loop(0, extra.shape[3] // (2 * SUB), body, 0, unroll=7)
            leave(x).start()

        copies += [leave(x) for x in range(depth)]
    for place in range(here):
        tile = first + place

        def squares(x):
            total = jnp.zeros((SUB, LANES), f32)
            for group in range(count // SUB):
                for a in range(3):
                    q = base[0, 0, tile, a, pl.ds(group * SUB, SUB), pl.ds(x * LANES, LANES)]
                    total = total + q * q
            return [total]

        sums = packed_sums(squares, depth)
        for step in range(2):
            relaxes[place, step] = relax_of(sums[0], inverse)

            def sums_of(x):
                lanes = pl.ds(x * LANES, LANES)
                matrix = with_diagonal(tile_grad(grad, depth, tile, x), wide(relaxes[place, step, pl.ds(x, 1), :]))

                def read(a, rows):
                    return base[0, 0, tile, a, rows, lanes] if step == 0 else halfway[place, a, rows, lanes]

                def write(a, rows, value):
                    if step == 0:
                        halfway[place, a, rows, lanes] = value
                    elif place < direct:
                        early[place, a, rows, lanes] = value
                    else:
                        fields[place - direct, a, rows, lanes] = value

                def shock(_, a, rows):
                    return noise[0, 0, tile, step, a, rows, lanes]

                if step == 0:
                    return tile_sums(read, write, shock, [matrix], count, add_square, 1)
                return tile_sums(read, write, shock, [matrix], count, add_moments, 6)

            sums = packed_sums(sums_of, depth)
        if place < direct:
            copies.append(pltpu.make_async_copy(early.at[place], new_base.at[0, 0, tile], sems.at[len(copies)]))
            copies[-1].start()
        for i, row in enumerate(stress_rows(sums, inverse)):
            stress[i, place] = row
    for copy in copies:
        copy.wait()


def call_ordinary(first, here, direct, before, base_fields, base_noise, grad, block, new_base, extra):
    count, cells = base_fields.shape[-2:]
    depth = cells // LANES
    has_block, has_base, has_extra = block is not None, new_base is not None, extra is not None
    operands = [before, *near_memory(base_fields, base_noise), grad]
    specs = [anywhere, vmem, vmem, vmem]
    shapes, out_specs, aliases = [], [], {}
    copies = 0
    if has_block:
        operands += near_memory(block)
        specs.append(vmem)
        copies += block.shape[0]
    if has_block or direct:
        copies += direct
        shapes.append(jax.ShapeDtypeStruct(base_fields.shape, f32))
        out_specs.append(hbm)
    if has_base:
        aliases[len(operands)] = 0
        operands.append(new_base)
        specs.append(hbm)
    if has_extra:
        operands += near_memory(*extra[:2]) + [extra[2]]
        specs += [vmem] * 3
        shapes.append(jax.ShapeDtypeStruct(extra[0].shape, f32))
        out_specs.append(hbm)
        copies += depth
    shapes += [
        pltpu.VMEM((here - direct, 3, count, cells), f32),
        jax.ShapeDtypeStruct((6, here, depth, LANES), f32),
    ]
    out_specs += [vmem, vmem]
    results = pl.pallas_call(
        functools.partial(ordinary, first, direct, has_block, has_base, has_extra),
        out_shape=tuple(shapes),
        in_specs=specs,
        out_specs=tuple(out_specs),
        input_output_aliases=aliases,
        scratch_shapes=[
            pltpu.VMEM((max(direct, 1), 3, count, cells), f32),
            pltpu.VMEM((here, 3, count, cells), f32),
            pltpu.VMEM((here, 2, depth, LANES), f32),
            pltpu.VMEM(extra[0].shape[2:] if has_extra else (SUB, LANES), f32),
            pltpu.SemaphoreType.DMA((max(copies, 1),)),
        ],
        compiler_params=pltpu.CompilerParams(vmem_limit_bytes=SMALL),
        cost_estimate=small(8 << 20, 3 << 20),
        name="ordinary_tiles",
    )(*operands)
    results = list(results)
    piece, block = results.pop(), results.pop()
    new_base = results.pop(0) if has_block or direct else None
    return new_base, block, piece, (results[0] if has_extra else None)


def moments_after(g, first, second, m):
    one, two = with_diagonal(g, first), with_diagonal(g, second)
    both = [[sum(two[3 * a + k] * one[3 * k + b] for k in range(3)) for b in range(3)] for a in range(3)]
    kick = [[noise_scale * two[3 * a + b] for b in range(3)] for a in range(3)]

    def mixed(of_q, of_w):
        return [
            [sum(both[a][i] * of_q(i, j) for i in range(3)) + sum(kick[a][i] * of_w(i, j) for i in range(3)) for j in range(3)]
            for a in range(3)
        ]

    with_q = mixed(lambda i, j: m[moment_of[i, j]], lambda i, j: m[6 + 3 * j + i])
    with_one = mixed(lambda i, j: m[6 + 3 * i + j], lambda i, j: m[15 + moment_of[i, j]])
    with_two = mixed(lambda i, j: m[21 + 3 * i + j], lambda i, j: m[30 + 3 * i + j])
    return [
        sum(with_q[a][j] * both[b][j] + with_one[a][j] * kick[b][j] for j in range(3))
        + noise_scale * (with_two[a][b] + with_two[b][a])
        + noise_scale**2 * m[39 + i]
        for i, (a, b) in enumerate(component_pairs)
    ]


def answering(before, moments, later, *refs):
    *parts, reply, drive = refs
    inverse = 1.0 / float(ALL_FIELDS)
    message = [sum(part[i] for part in parts) for i in range(12)]
    grad, m = message[:9], [moments[i] for i in range(21)] + [later[i] for i in range(24)]
    own = coefficients(grad, m[:15] + [m[15] + m[16] + m[17]])
    both = [message[9 + i] + own[i] for i in range(3)]
    first = relax_of(both[2], inverse)
    second = relax_of(both[0] + first * (both[1] + first * both[2]), inverse)
    for i, value in enumerate([first, second] + moments_after(grad, first, second, m)):
        reply[i] = value
    for i, value in enumerate(grad + [first, second]):
        drive[i] = value


def call_answering(before, moments, later, parts):
    depth = moments.shape[1]
    return pl.pallas_call(
        answering,
        out_shape=(
            jax.ShapeDtypeStruct((8, depth, LANES), f32),
            jax.ShapeDtypeStruct((11, depth, LANES), f32),
        ),
        in_specs=[anywhere] + [vmem] * (2 + len(parts)),
        out_specs=(vmem, vmem),
        compiler_params=pltpu.CompilerParams(vmem_limit_bytes=4 << 20),
        cost_estimate=small(1 << 20, 1 << 19),
        name="answering",
    )(before, moments, later, *parts)


def heavy(parity, helper, base, noise, grad, replies, new_base, rows, fields, answer, sems):
    _, _, tiles, _, count, cells = base.shape
    me = lax.axis_index("gy")
    depth = cells // LANES
    flat = rows.reshape(6 * depth * tiles, LANES)

    def store(k, tile):
        return pltpu.make_async_copy(fields.at[k], new_base.at[0, 0, tile], sems.at[k])

    places, order = owned_order(tiles, me, helper, (parity,))
    for k, (h, tile) in enumerate(order):

        @pl.when(k < places)
        def _(k=k, h=h, tile=tile):
            answer[...] = replies[(me ^ h) >> 1]

            def sums_of(x):
                lanes = pl.ds(x * LANES, LANES)
                g = tile_grad(grad, depth, tile, x)
                matrices = [with_diagonal(g, wide(answer[step, pl.ds(x, 1), :])) for step in range(2)]

                def read(a, part):
                    return base[0, 0, tile, a, part, lanes]

                def write(a, part, value):
                    fields[k, a, part, lanes] = value

                def shock(step, a, part):
                    return noise[0, 0, tile, step, a, part, lanes]

                return tile_sums(read, write, shock, matrices, count, add_moments, 6)

            sums = packed_sums(sums_of, depth)
            store(k, tile).start()
            sums = [s + answer[2 + i] for i, s in enumerate(sums)]
            for i, value in enumerate(stress_rows(sums, 1.0 / ALL_FIELDS)):
                flat[pl.ds(i * depth * tiles + tile, depth, stride=tiles), :] = value

    def wait():
        for k, (_, tile) in enumerate(order):

            @pl.when(k < places)
            def _(k=k, tile=tile):
                store(k, tile).wait()

    return wait


def heavy_scratch(near, held):
    return [pltpu.VMEM((HEAVY_MOST,) + held, f32), pltpu.VMEM(near.shape[1:], f32)]


def finish(piece_count, helper, base, noise, grad, near, block, *refs):
    pieces, (_, new_base, rows, fields, answer, sems) = refs[:piece_count], refs[piece_count:]
    _, depth, tiles, _ = rows.shape
    last = block.shape[0]
    flat = rows.reshape(6 * depth * tiles, LANES)
    me = lax.axis_index("gy")
    named = [jnp.bool_(False)] * last
    for _, owned, tile in owned_slots(tiles, me, helper):
        named = [n | (owned & (tile == tiles - last + i)) for i, n in enumerate(named)]
    copies = [
        pltpu.make_async_copy(block.at[i], new_base.at[0, 0, tiles - last + i], sems.at[HEAVY_MOST + i])
        for i in range(last)
    ]
    for copy, is_heavy in zip(copies, named):
        pl.when(jnp.logical_not(is_heavy))(copy.start)
    tile = 0
    for piece in pieces:
        for place in range(piece.shape[1]):
            for i in range(6):
                flat[pl.ds(i * depth * tiles + tile, depth, stride=tiles), :] = piece[i, place]
            tile += 1
    wait = heavy(0, helper, base, noise, grad, near, new_base, rows, fields, answer, sems)
    wait()
    for copy, is_heavy in zip(copies, named):
        pl.when(jnp.logical_not(is_heavy))(copy.wait)


def call_finish(helper_tile, base_fields, base_noise, grad, near, block, pieces, new_base):
    tiles, cells = new_base.shape[2], new_base.shape[-1]
    return pl.pallas_call(
        functools.partial(finish, len(pieces)),
        out_shape=(
            jax.ShapeDtypeStruct(new_base.shape, f32),
            jax.ShapeDtypeStruct((6, cells // LANES, tiles, LANES), f32),
        ),
        in_specs=[vmem] * (6 + len(pieces)) + [hbm],
        out_specs=(hbm, vmem),
        input_output_aliases={6 + len(pieces): 0},
        scratch_shapes=heavy_scratch(near, block.shape[1:])
        + [pltpu.SemaphoreType.DMA((HEAVY_MOST + block.shape[0],))],
        compiler_params=pltpu.CompilerParams(vmem_limit_bytes=SMALL),
        cost_estimate=small(1 << 10, 1 << 20),
        name="finish",
    )(helper_tile, *near_memory(base_fields, base_noise), grad, near, *near_memory(block), *pieces, new_base)


def final(helper, base, noise, grad, far, ready, old_base, new_base, stress, rows, fields, answer, sems):
    depth = rows.shape[1]

    def result(x):
        target = stress.at[0, 0, :, :, pl.ds(x * LANES, LANES)]
        return pltpu.make_async_copy(rows.at[:, x], target, sems.at[HEAVY_MOST + x])

    rows[...] = ready[...]
    wait = heavy(1, helper, base, noise, grad, far, new_base, rows, fields, answer, sems)
    for x in range(depth):
        result(x).start()
    wait()
    for x in range(depth):
        result(x).wait()


def call_final(helper_tile, base_fields, base_noise, grad, far, ready, new_base):
    _, _, tiles, _, count, cells = base_fields.shape
    depth = cells // LANES
    return pl.pallas_call(
        final,
        out_shape=(
            jax.ShapeDtypeStruct(new_base.shape, f32),
            jax.ShapeDtypeStruct((1, 1, 6, tiles, cells), f32),
        ),
        in_specs=[vmem] * 6 + [hbm],
        out_specs=(hbm, hbm),
        input_output_aliases={6: 0},
        scratch_shapes=[pltpu.VMEM((6, depth, tiles, LANES), f32)]
        + heavy_scratch(far, (3, count, cells))
        + [pltpu.SemaphoreType.DMA((HEAVY_MOST + depth,))],
        compiler_params=pltpu.CompilerParams(vmem_limit_bytes=SMALL),
        cost_estimate=small(8 << 20, 4 << 20),
        name="heavy_tiles",
    )(helper_tile, *near_memory(base_fields, base_noise), grad, far, ready, new_base)


def per_device(
    velocity, wall_cells, tile_counts, helper_tile, base_fields, extra_fields, base_noise, extra_noise
):
    tiles = tile_counts.shape[2]
    pairs = lax.axis_size("gy") // 2
    helper_tile, x_one, x_two, y_one, y_two = call_edges(helper_tile, velocity)
    y_two = swap_across(y_two, False)
    x_two = swap_across(x_two, True)
    x_one = swap_within(x_one, "gx")
    y_one = swap_within(y_one, "gy")
    halos = (y_two, x_two, x_one, y_one)
    moments = call_heavy_moments(helper_tile, base_fields, base_noise)
    later = call_extra_moments(2, moments, extra_fields, extra_noise)
    grad, keep, send = call_gradients(tiles, later, helper_tile, velocity, halos, wall_cells, moments)
    some = 3 * tiles // 8
    ordinary_fields = (base_fields, base_noise, grad)
    received = swapped(send, 1)
    _, block, begun, _ = call_ordinary(0, some, 0, send, *ordinary_fields, None, None, None)
    keep, *sends = call_merge(begun, keep, received)
    farthest_first = sorted(range(1, pairs), key=lambda flip: -flip.bit_count())
    parts = [keep] + [swapped(sends[flip - 1], 2 * flip) for flip in farthest_first]
    extra_sums = call_extra_moments(1, sends[0], extra_fields, extra_noise)
    more = tiles - some - 3
    new_base, block, going, _ = call_ordinary(some, more, 0, extra_sums, *ordinary_fields, block, None, None)
    reply, drive = call_answering(going, extra_sums, later, parts)
    replies = {flip: swapped(reply, 2 * flip) for flip in farthest_first}
    new_base, block, ended, new_extra = call_ordinary(
        tiles - 3, 3, 1, reply, *ordinary_fields, block, new_base, (extra_fields, extra_noise, drive)
    )
    near = call_join(ended, [reply] + [replies[flip] for flip in range(1, pairs)])
    far = swapped(near, 1)
    given = (helper_tile, base_fields, base_noise, grad)
    new_base, ready = call_finish(*given, near, block, (begun, going, ended), new_base)
    new_base, stress = call_final(*given, far, ready, new_base)
    return new_base, new_extra, jnp.swapaxes(stress, 2, 3)


def solution(mesh):
    in_specs = (
        P(None, "gx", "gy", None),
        P("gx", "gy", None),
        P("gx", "gy", None),
        P("gx", None),
        P("gx", "gy", None, None, None, None),
        P("gx", "gy", None, None, None),
        P("gx", "gy", None, None, None, None, None),
        P("gx", "gy", None, None, None, None),
    )
    out_specs = (
        P("gx", "gy", None, None, None, None),
        P("gx", "gy", None, None, None),
        P("gx", "gy", None, None, None),
    )
    return jax.shard_map(
        per_device, mesh=mesh, in_specs=in_specs, out_specs=out_specs, check_vma=False
    )
```

profile of v0, /device:TPU:0, one launch (start us, length us, event | category | flops | bytes accessed | tf_op | source)
XLA Modules:
  0.0 31.2 jit_solution(17810570214081959644)
XLA Ops:
  0.6 0.9 %edges.1 = (s32[1,8]{1,0:T(1,128)S(1)}, f32[3,8,128]{2,1,0:T(8,128)S(1)}, f32[3,8,128]{2,1,0:T(8,128)S(1)}, f32[3,8,128]{2,1,0:T(8,128)S(1)}, f32[3,8,128]{2,1,0:T(8,128)S(1)}) custom-call(s32[1,8]{1,0:T(1,128)} %helper.1, f32[3,8,8,128]{3,2,1,0:T(8,128)} %velocity.3), custom_call_target="tpu_custom_call" | custom-call | flops 1024 | bytes 131072 | tf_op jit(solution)/shard_map/edges/pallas_call | solution.py:172
  1.6 3.1 %collective-permute-start = (f32[3,8,128]{2,1,0:T(8,128)S(1)}, f32[3,8,128]{2,1,0:T(8,128)S(1)}, u32[]{:S(2)}, u32[]{:S(2)}) collective-permute-start(f32[3,8,128]{2,1,0:T(8,128)S(1)} %get-tuple-element.31), channel_id=1, source_target_pairs={{0,8},{1,2},{2,1},{3,4},{4,3},{5,6},{6,5},{7,15},{8,0},{9,10},{10,... | collective-permute-start | bytes 36872 | tf_op jit(solution)/shard_map/ppermute | solution.py:201
  4.7 0.0 collective-permute-start.1
  4.7 3.1 %collective-permute-start.2 = (f32[3,8,128]{2,1,0:T(8,128)S(1)}, f32[3,8,128]{2,1,0:T(8,128)S(1)}, u32[]{:S(2)}, u32[]{:S(2)}) collective-permute-start(f32[3,8,128]{2,1,0:T(8,128)S(1)} %get-tuple-element.33), channel_id=1, source_target_pairs={{0,8},{8,0},{16,24},{24,16},{1,9},{9,1},{17,25},{25,17},{2,10},{10... | collective-permute-start | bytes 36872 | tf_op jit(solution)/shard_map/ppermute | solution.py:184
  7.8 0.0 collective-permute-start.3
  7.8 0.0 copy-start.5
  7.8 0.3 heavy_moments.1.before.moments
  8.1 1.5 %copy-done.2 = f32[1,1,3,224,1024]{4,3,2,1,0:T(8,128)S(1)} copy-done((f32[1,1,3,224,1024]{4,3,2,1,0:T(8,128)S(1)}, f32[1,1,3,224,1024]{4,3,2,1,0:T(8,128)}, u32[]{:S(2)}) %copy-start.2) | copy-done | bytes 2752536
  9.6 0.8 %copy-done.3 = bf16[1,1,2,3,224,1024]{5,4,3,2,1,0:T(8,128)(2,1)S(1)} copy-done((bf16[1,1,2,3,224,1024]{5,4,3,2,1,0:T(8,128)(2,1)S(1)}, bf16[1,1,2,3,224,1024]{5,4,3,2,1,0:T(8,128)(2,1)}, u32[]{:S(2)}) %copy-start.3) | copy-done | bytes 2752536
  10.4 1.9 %extra_moments.2.before.later = f32[24,8,128]{2,1,0:T(8,128)S(1)} custom-call(f32[8,16,8,128]{3,2,1,0:T(8,128)S(1)} %heavy_moments.1.before.moments, f32[1,1,3,224,1024]{4,3,2,1,0:T(8,128)S(1)} %copy-done.2, bf16[1,1,2,3,224,1024]{5,4,3,2,1,0:T(8,128)(2,1)S(1)} %copy-done.3), custom_call_target="tpu_custom_call" | custom-call | flops 8388608 | bytes 5242880 | tf_op jit(solution)/shard_map/extra_moments/pallas_call | solution.py:305
  12.4 0.0 collective-permute-done.1.x_two
  12.4 0.0 collective-permute-done.2.x_one
  12.4 0.7 %gradients.1 = (f32[576,128]{1,0:T(8,128)S(1)}, f32[4,12,8,128]{3,2,1,0:T(8,128)S(1)}, f32[4,12,8,128]{3,2,1,0:T(8,128)S(1)}) custom-call(f32[24,8,128]{2,1,0:T(8,128)S(1)} %extra_moments.2.before.later, s32[1,8]{1,0:T(1,128)S(1)} %get-tuple-element.30.helper, f32[3,8,8,128]{3,2,1,0:T(8,128)S(1)} %copy-done.4, f32[3,8,128]{2,1,0:T(8,128)S(1)} %collective-permute-done.y_two, ...), custom_call_target="tpu_custom_call" | custom-call | flops 4194304 | bytes 1048576 | tf_op jit(solution)/shard_map/gradients/pallas_call | solution.py:370
  13.1 0.6 %collective-permute-start.4 = (f32[4,12,8,128]{3,2,1,0:T(8,128)S(1)}, f32[4,12,8,128]{3,2,1,0:T(8,128)S(1)}, u32[]{:S(2)}, u32[]{:S(2)}) collective-permute-start(f32[4,12,8,128]{3,2,1,0:T(8,128)S(1)} %get-tuple-element.36.refs_0_), channel_id=1, source_target_pairs={{0,1},{1,0},{2,3},{3,2},{4,5},{5,4},{6,7},{7,6},{8,9},{9,8},{10,11... | collective-permute-start | bytes 589832 | tf_op jit(solution)/shard_map/ppermute | solution.py:383
  13.7 1.1 %ordinary_tiles.3 = (f32[3,3,32,1024]{3,2,1,0:T(8,128)S(1)}, f32[6,3,8,128]{3,2,1,0:T(8,128)S(1)}) custom-call(f32[4,12,8,128]{3,2,1,0:T(8,128)S(1)} %get-tuple-element.36.refs_0_, f32[1,1,8,3,32,1024]{5,4,3,2,1,0:T(8,128)S(1)} %copy-done, bf16[1,1,8,2,3,32,1024]{6,5,4,3,2,1,0:T(8,128)(2,1)S(1)} %copy-done.1, f32[576,128]{1,0:T(8,128)S(1)} %get-tuple-element.35.refs_3_.grad), custom_call_target="tpu_custom_call" | custom-call | flops 8388608 | bytes 3145728 | tf_op jit(solution)/shard_map/ordinary_tiles/pallas_call | solution.py:583
  14.8 0.0 collective-permute-done.4.received
  14.9 1.3 %collective-permute-start.5 = (f32[12,8,128]{2,1,0:T(8,128)S(1)}, f32[12,8,128]{2,1,0:T(8,128)S(1)}, u32[]{:S(2)}, u32[]{:S(2)}) collective-permute-start(f32[12,8,128]{2,1,0:T(8,128)S(1)} %get-tuple-element.43), channel_id=1, source_target_pairs={{0,6},{1,7},{2,4},{3,5},{4,2},{5,3},{6,0},{7,1},{8,14},{9,15},{10,... | collective-permute-start | bytes 147464 | tf_op jit(solution)/shard_map/ppermute | solution.py:383
  16.1 1.8 %collective-permute-start.6 = (f32[12,8,128]{2,1,0:T(8,128)S(1)}, f32[12,8,128]{2,1,0:T(8,128)S(1)}, u32[]{:S(2)}, u32[]{:S(2)}) collective-permute-start(f32[12,8,128]{2,1,0:T(8,128)S(1)} %get-tuple-element.39.before), channel_id=1, source_target_pairs={{0,2},{1,3},{2,0},{3,1},{4,6},{5,7},{6,4},{7,5},{8,10},{9,11},{10,... | collective-permute-start | bytes 147464 | tf_op jit(solution)/shard_map/ppermute | solution.py:383
  18.0 0.4 %collective-permute-start.7 = (f32[12,8,128]{2,1,0:T(8,128)S(1)}, f32[12,8,128]{2,1,0:T(8,128)S(1)}, u32[]{:S(2)}, u32[]{:S(2)}) collective-permute-start(f32[12,8,128]{2,1,0:T(8,128)S(1)} %get-tuple-element.44), channel_id=1, source_target_pairs={{0,4},{1,5},{2,6},{3,7},{4,0},{5,1},{6,2},{7,3},{8,12},{9,13},{10,... | collective-permute-start | bytes 147464 | tf_op jit(solution)/shard_map/ppermute | solution.py:383
  18.4 1.6 %extra_moments.3.refs_0_.moments = f32[21,8,128]{2,1,0:T(8,128)S(1)} custom-call(f32[12,8,128]{2,1,0:T(8,128)S(1)} %get-tuple-element.39.before, f32[1,1,3,224,1024]{4,3,2,1,0:T(8,128)S(1)} %copy-done.2, bf16[1,1,2,3,224,1024]{5,4,3,2,1,0:T(8,128)(2,1)S(1)} %copy-done.3), custom_call_target="tpu_custom_call" | custom-call | flops 8388608 | bytes 5242880 | tf_op jit(solution)/shard_map/extra_moments/pallas_call | solution.py:305
  20.0 1.0 %ordinary_tiles.4 = (f32[1,1,8,3,32,1024]{5,4,3,2,1,0:T(8,128)}, f32[2,3,32,1024]{3,2,1,0:T(8,128)S(1)}, f32[6,2,8,128]{3,2,1,0:T(8,128)S(1)}) custom-call(f32[21,8,128]{2,1,0:T(8,128)S(1)} %extra_moments.3.refs_0_.moments, f32[1,1,8,3,32,1024]{5,4,3,2,1,0:T(8,128)S(1)} %copy-done, bf16[1,1,8,2,3,32,1024]{6,5,4,3,2,1,0:T(8,128)(2,1)S(1)} %copy-done.1, ...), custom_call_target="tpu_custom_call" | custom-call | flops 8388608 | bytes 3145728 | tf_op jit(solution)/shard_map/ordinary_tiles/pallas_call | solution.py:583
  21.1 0.0 collective-permute-done.5.refs_1_
  21.1 1.0 %collective-permute-done.7.refs_3_ = f32[12,8,128]{2,1,0:T(8,128)S(1)} collective-permute-done((f32[12,8,128]{2,1,0:T(8,128)S(1)}, f32[12,8,128]{2,1,0:T(8,128)S(1)}, u32[]{:S(2)}, u32[]{:S(2)}) %collective-permute-start.7) | collective-permute-done | bytes 49184 | tf_op jit(solution)/shard_map/ppermute | solution.py:383
  22.1 0.1 answering.1
  22.2 0.9 %collective-permute-start.10 = (f32[8,8,128]{2,1,0:T(8,128)S(1)}, f32[8,8,128]{2,1,0:T(8,128)S(1)}, u32[]{:S(2)}, u32[]{:S(2)}) collective-permute-start(f32[8,8,128]{2,1,0:T(8,128)S(1)} %get-tuple-element.45.refs_0_), channel_id=1, source_target_pairs={{0,6},{1,7},{2,4},{3,5},{4,2},{5,3},{6,0},{7,1},{8,14},{9,15},{10,... | collective-permute-start | bytes 98312 | tf_op jit(solution)/shard_map/ppermute | solution.py:383
  23.1 1.2 %collective-permute-start.8 = (f32[8,8,128]{2,1,0:T(8,128)S(1)}, f32[8,8,128]{2,1,0:T(8,128)S(1)}, u32[]{:S(2)}, u32[]{:S(2)}) collective-permute-start(f32[8,8,128]{2,1,0:T(8,128)S(1)} %get-tuple-element.45.refs_0_), channel_id=1, source_target_pairs={{0,2},{1,3},{2,0},{3,1},{4,6},{5,7},{6,4},{7,5},{8,10},{9,11},{10,... | collective-permute-start | bytes 98312 | tf_op jit(solution)/shard_map/ppermute | solution.py:383
  24.3 1.4 %collective-permute-start.9 = (f32[8,8,128]{2,1,0:T(8,128)S(1)}, f32[8,8,128]{2,1,0:T(8,128)S(1)}, u32[]{:S(2)}, u32[]{:S(2)}) collective-permute-start(f32[8,8,128]{2,1,0:T(8,128)S(1)} %get-tuple-element.45.refs_0_), channel_id=1, source_target_pairs={{0,4},{1,5},{2,6},{3,7},{4,0},{5,1},{6,2},{7,3},{8,12},{9,13},{10,... | collective-permute-start | bytes 98312 | tf_op jit(solution)/shard_map/ppermute | solution.py:383
  25.7 3.0 %ordinary_tiles.5 = (f32[1,1,8,3,32,1024]{5,4,3,2,1,0:T(8,128)}, f32[1,1,3,224,1024]{4,3,2,1,0:T(8,128)}, f32[2,3,32,1024]{3,2,1,0:T(8,128)S(1)}, f32[6,3,8,128]{3,2,1,0:T(8,128)S(1)}) custom-call(f32[8,8,128]{2,1,0:T(8,128)S(1)} %get-tuple-element.45.refs_0_, f32[1,1,8,3,32,1024]{5,4,3,2,1,0:T(8,128)S(1)} %copy-done, ...), custom_call_target="tpu_custom_call", output_to_operand_aliasing={{0}: (5, {})} | custom-call | flops 8388608 | bytes 3145728 | tf_op jit(solution)/shard_map/ordinary_tiles/pallas_call | solution.py:583
  28.8 0.1 collective-permute-start.11
  28.9 1.1 %finish.1 = (f32[1,1,8,3,32,1024]{5,4,3,2,1,0:T(8,128)}, f32[6,8,8,128]{3,2,1,0:T(8,128)S(1)}) custom-call(s32[1,8]{1,0:T(1,128)S(1)} %get-tuple-element.30.helper, f32[1,1,8,3,32,1024]{5,4,3,2,1,0:T(8,128)S(1)} %copy-done, bf16[1,1,8,2,3,32,1024]{6,5,4,3,2,1,0:T(8,128)(2,1)S(1)} %copy-done.1, ...), custom_call_target="tpu_custom_call", output_to_operand_aliasing={{0}: (9, {})} | custom-call | flops 1024 | bytes 1048576 | tf_op jit(solution)/shard_map/finish/pallas_call | solution.py:740
  30.0 0.2 collective-permute-done.11.far
  30.2 1.0 %heavy_tiles.1 = (f32[1,1,8,3,32,1024]{5,4,3,2,1,0:T(8,128)}, f32[1,1,6,8,1024]{4,3,2,1,0:T(8,128)}) custom-call(s32[1,8]{1,0:T(1,128)S(1)} %get-tuple-element.30.helper, f32[1,1,8,3,32,1024]{5,4,3,2,1,0:T(8,128)S(1)} %copy-done, bf16[1,1,8,2,3,32,1024]{6,5,4,3,2,1,0:T(8,128)(2,1)S(1)} %copy-done.1, ...), custom_call_target="tpu_custom_call", output_to_operand_aliasing={{0}: (6, {})} | custom-call | flops 8388608 | bytes 4194304 | tf_op jit(solution)/shard_map/heavy_tiles/pallas_call | solution.py:776
  (17 shorter events, 0.1 us)
Async XLA Ops:
  1.6 10.8 %collective-permute-start = (f32[3,8,128]{2,1,0:T(8,128)S(1)}, f32[3,8,128]{2,1,0:T(8,128)S(1)}, u32[]{:S(2)}, u32[]{:S(2)}) collective-permute-start(f32[3,8,128]{2,1,0:T(8,128)S(1)} %get-tuple-element.31), channel_id=1, source_target_pairs={{0,8},{1,2},{2,1},{3,4},{4,3},{5,6},{6,5},{7,15},{8,0},{9,10},{10,... | collective-permute-start | bytes 36872 | tf_op jit(solution)/shard_map/ppermute | solution.py:201
  4.7 7.7 %collective-permute-start.1 = (f32[3,8,128]{2,1,0:T(8,128)S(1)}, f32[3,8,128]{2,1,0:T(8,128)S(1)}, u32[]{:S(2)}, u32[]{:S(2)}) collective-permute-start(f32[3,8,128]{2,1,0:T(8,128)S(1)} %get-tuple-element.32), channel_id=1, source_target_pairs={{0,1},{1,0},{2,3},{3,2},{4,5},{5,4},{6,7},{7,6},{8,16},{9,17},{10,... | collective-permute-start | bytes 36872 | tf_op jit(solution)/shard_map/ppermute | solution.py:201
  4.7 7.7 %collective-permute-start.2 = (f32[3,8,128]{2,1,0:T(8,128)S(1)}, f32[3,8,128]{2,1,0:T(8,128)S(1)}, u32[]{:S(2)}, u32[]{:S(2)}) collective-permute-start(f32[3,8,128]{2,1,0:T(8,128)S(1)} %get-tuple-element.33), channel_id=1, source_target_pairs={{0,8},{8,0},{16,24},{24,16},{1,9},{9,1},{17,25},{25,17},{2,10},{10... | collective-permute-start | bytes 36872 | tf_op jit(solution)/shard_map/ppermute | solution.py:184
  7.8 4.6 %collective-permute-start.3 = (f32[3,8,128]{2,1,0:T(8,128)S(1)}, f32[3,8,128]{2,1,0:T(8,128)S(1)}, u32[]{:S(2)}, u32[]{:S(2)}) collective-permute-start(f32[3,8,128]{2,1,0:T(8,128)S(1)} %get-tuple-element.34), channel_id=1, source_target_pairs={{0,1},{1,0},{2,3},{3,2},{4,5},{5,4},{6,7},{7,6},{8,9},{9,8},{10,11... | collective-permute-start | bytes 36872 | tf_op jit(solution)/shard_map/ppermute | solution.py:184
  7.8 1.8 %copy-start.2 = (f32[1,1,3,224,1024]{4,3,2,1,0:T(8,128)S(1)}, f32[1,1,3,224,1024]{4,3,2,1,0:T(8,128)}, u32[]{:S(2)}) copy-start(f32[1,1,3,224,1024]{4,3,2,1,0:T(8,128)} %refs_6_.1) | copy-start | bytes 8257540
  7.8 2.6 %copy-start.3 = (bf16[1,1,2,3,224,1024]{5,4,3,2,1,0:T(8,128)(2,1)S(1)}, bf16[1,1,2,3,224,1024]{5,4,3,2,1,0:T(8,128)(2,1)}, u32[]{:S(2)}) copy-start(bf16[1,1,2,3,224,1024]{5,4,3,2,1,0:T(8,128)(2,1)} %refs_7_.1) | copy-start | bytes 8257540
  7.8 4.6 %copy-start.4 = (f32[3,8,8,128]{3,2,1,0:T(8,128)S(1)}, f32[3,8,8,128]{3,2,1,0:T(8,128)}, u32[]{:S(2)}) copy-start(f32[3,8,8,128]{3,2,1,0:T(8,128)} %velocity.3) | copy-start | bytes 294916
  7.8 4.6 %copy-start.5 = (s32[8,8,128]{2,1,0:T(8,128)S(1)}, s32[8,8,128]{2,1,0:T(8,128)}, u32[]{:S(2)}) copy-start(s32[8,8,128]{2,1,0:T(8,128)} %wall.1) | copy-start | bytes 98308
  10.4 3.2 %copy-start = (f32[1,1,8,3,32,1024]{5,4,3,2,1,0:T(8,128)S(1)}, f32[1,1,8,3,32,1024]{5,4,3,2,1,0:T(8,128)}, u32[]{:S(2)}) copy-start(f32[1,1,8,3,32,1024]{5,4,3,2,1,0:T(8,128)} %base.9) | copy-start | bytes 9437188
  10.4 3.2 %copy-start.1 = (bf16[1,1,8,2,3,32,1024]{6,5,4,3,2,1,0:T(8,128)(2,1)S(1)}, bf16[1,1,8,2,3,32,1024]{6,5,4,3,2,1,0:T(8,128)(2,1)}, u32[]{:S(2)}) copy-start(bf16[1,1,8,2,3,32,1024]{6,5,4,3,2,1,0:T(8,128)(2,1)} %noise.9) | copy-start | bytes 9437188
  13.1 1.7 %collective-permute-start.4 = (f32[4,12,8,128]{3,2,1,0:T(8,128)S(1)}, f32[4,12,8,128]{3,2,1,0:T(8,128)S(1)}, u32[]{:S(2)}, u32[]{:S(2)}) collective-permute-start(f32[4,12,8,128]{3,2,1,0:T(8,128)S(1)} %get-tuple-element.36.refs_0_), channel_id=1, source_target_pairs={{0,1},{1,0},{2,3},{3,2},{4,5},{5,4},{6,7},{7,6},{8,9},{9,8},{10,11... | collective-permute-start | bytes 589832 | tf_op jit(solution)/shard_map/ppermute | solution.py:383
  14.9 6.2 %collective-permute-start.5 = (f32[12,8,128]{2,1,0:T(8,128)S(1)}, f32[12,8,128]{2,1,0:T(8,128)S(1)}, u32[]{:S(2)}, u32[]{:S(2)}) collective-permute-start(f32[12,8,128]{2,1,0:T(8,128)S(1)} %get-tuple-element.43), channel_id=1, source_target_pairs={{0,6},{1,7},{2,4},{3,5},{4,2},{5,3},{6,0},{7,1},{8,14},{9,15},{10,... | collective-permute-start | bytes 147464 | tf_op jit(solution)/shard_map/ppermute | solution.py:383
  16.1 4.9 %collective-permute-start.6 = (f32[12,8,128]{2,1,0:T(8,128)S(1)}, f32[12,8,128]{2,1,0:T(8,128)S(1)}, u32[]{:S(2)}, u32[]{:S(2)}) collective-permute-start(f32[12,8,128]{2,1,0:T(8,128)S(1)} %get-tuple-element.39.before), channel_id=1, source_target_pairs={{0,2},{1,3},{2,0},{3,1},{4,6},{5,7},{6,4},{7,5},{8,10},{9,11},{10,... | collective-permute-start | bytes 147464 | tf_op jit(solution)/shard_map/ppermute | solution.py:383
  18.0 4.1 %collective-permute-start.7 = (f32[12,8,128]{2,1,0:T(8,128)S(1)}, f32[12,8,128]{2,1,0:T(8,128)S(1)}, u32[]{:S(2)}, u32[]{:S(2)}) collective-permute-start(f32[12,8,128]{2,1,0:T(8,128)S(1)} %get-tuple-element.44), channel_id=1, source_target_pairs={{0,4},{1,5},{2,6},{3,7},{4,0},{5,1},{6,2},{7,3},{8,12},{9,13},{10,... | collective-permute-start | bytes 147464 | tf_op jit(solution)/shard_map/ppermute | solution.py:383
  22.2 6.5 %collective-permute-start.10 = (f32[8,8,128]{2,1,0:T(8,128)S(1)}, f32[8,8,128]{2,1,0:T(8,128)S(1)}, u32[]{:S(2)}, u32[]{:S(2)}) collective-permute-start(f32[8,8,128]{2,1,0:T(8,128)S(1)} %get-tuple-element.45.refs_0_), channel_id=1, source_target_pairs={{0,6},{1,7},{2,4},{3,5},{4,2},{5,3},{6,0},{7,1},{8,14},{9,15},{10,... | collective-permute-start | bytes 98312 | tf_op jit(solution)/shard_map/ppermute | solution.py:383
  23.1 5.7 %collective-permute-start.8 = (f32[8,8,128]{2,1,0:T(8,128)S(1)}, f32[8,8,128]{2,1,0:T(8,128)S(1)}, u32[]{:S(2)}, u32[]{:S(2)}) collective-permute-start(f32[8,8,128]{2,1,0:T(8,128)S(1)} %get-tuple-element.45.refs_0_), channel_id=1, source_target_pairs={{0,2},{1,3},{2,0},{3,1},{4,6},{5,7},{6,4},{7,5},{8,10},{9,11},{10,... | collective-permute-start | bytes 98312 | tf_op jit(solution)/shard_map/ppermute | solution.py:383
  24.3 4.4 %collective-permute-start.9 = (f32[8,8,128]{2,1,0:T(8,128)S(1)}, f32[8,8,128]{2,1,0:T(8,128)S(1)}, u32[]{:S(2)}, u32[]{:S(2)}) collective-permute-start(f32[8,8,128]{2,1,0:T(8,128)S(1)} %get-tuple-element.45.refs_0_), channel_id=1, source_target_pairs={{0,4},{1,5},{2,6},{3,7},{4,0},{5,1},{6,2},{7,3},{8,12},{9,13},{10,... | collective-permute-start | bytes 98312 | tf_op jit(solution)/shard_map/ppermute | solution.py:383
  28.8 1.4 %collective-permute-start.11 = (f32[4,8,8,128]{3,2,1,0:T(8,128)S(1)}, f32[4,8,8,128]{3,2,1,0:T(8,128)S(1)}, u32[]{:S(2)}, u32[]{:S(2)}) collective-permute-start(f32[4,8,8,128]{3,2,1,0:T(8,128)S(1)} %join.1.near), channel_id=1, source_target_pairs={{0,1},{1,0},{2,3},{3,2},{4,5},{5,4},{6,7},{7,6},{8,9},{9,8},{10,11... | collective-permute-start | bytes 393224 | tf_op jit(solution)/shard_map/ppermute | solution.py:383
where the time goes:
time: 31.3 us; the launch traced here: 31.2 us
  starting transfers between devices  14 us (45%)
  Pallas kernels  12.8 us (41%)
  local copies, waits for them, and re-layouts  2.33 us (7%)
  waiting for transfers between devices  1.2 us (4%)
  between operations  0.84 us (3%)
    ppermute x8, starting transfers between devices, swapped(): return lax.ppermute(block, 'gy', [(i, i ^ flip) for i in range(size)])  7.75 us
    pallas_call x3, Pallas kernels, call_ordinary(): pl.pallas_call(functools.partial(ordinary, first, direct, has_block, has_...  5.15 us
    pallas_call x2, Pallas kernels, call_extra_moments(): pl.pallas_call(functools.partial(extra_moments, steps, 7), out_shape=jax....  3.51 us
    ppermute x2, starting transfers between devices, swap_within(): lax.ppermute(block, axis, [(i, i ^ 1) for i in range(lax.axis_size(axis))])  3.13 us
    ppermute x2, starting transfers between devices, swap_across(): lax.ppermute(block, ('gx', 'gy'), [(i, partner(*place)) for i, place in e...  3.12 us
    unnamed x12, local copies, waits for them, and re-layouts  2.33 us
    ppermute x8, waiting for transfers between devices, swapped(): return lax.ppermute(block, 'gy', [(i, i ^ flip) for i in range(size)])  1.19 us
    pallas_call x1, Pallas kernels, call_finish(): pl.pallas_call(functools.partial(finish, len(pieces)), out_shape=(jax.Sha...  1.14 us
  transfers between devices with their start and end apart: 12, of which 2 were waited for; matrix products, arithmetic and copies ran while one was open for 0% of the time, Pallas kernels for 32%

commit v1 on v0

--- a/solution.py
+++ b/solution.py
@@ -208,9 +208,16 @@
     return jnp.where(place == 0, 0.0, low), jnp.where(place == lax.axis_size(axis) - 1, 0.0, high)
 
 
-def heavy_moments(helper, base, noise, out, fields, shocks, sems):
+def later_sums(sums, q, one, two):
+    return outer_sums(sums[:9], q, two) + outer_sums(sums[9:18], one, two) + add_moments(sums[18:], two)
+
+
+def early_sums(helper, base, noise, extra, extra_noise, out, later, fields, shocks, near, near_noise, partial, sems):
     _, _, count, cells = fields.shape
+    depth = cells // LANES
     tiles = base.shape[2]
+    each = 4 * SUB
+    pieces = near.shape[1] // each
     me = lax.axis_index("gy")
 
     def loads(k, tile):
@@ -219,6 +226,13 @@
             pltpu.make_async_copy(noise.at[0, 0, tile, 0], shocks.at[k], sems.at[1, k]),
         )
 
+    def piece_loads(r):
+        rows = pl.ds(pl.multiple_of(r * each, each), each)
+        return (
+            pltpu.make_async_copy(extra.at[0, 0, :, rows], near.at[:, rows], sems.at[0, HEAVY_MOST + r]),
+            pltpu.make_async_copy(extra_noise.at[0, 0, :, :, rows], near_noise.at[:, :, rows], sems.at[1, HEAVY_MOST + r]),
+        )
+
     places, order = owned_order(tiles, me, helper)
     for k, (_, tile) in enumerate(order):
 
@@ -227,6 +241,10 @@
             for copy in loads(k, tile):
                 copy.start()
 
+    for r in range(pieces):
+        for copy in piece_loads(r):
+            copy.start()
+    partial[...] = jnp.zeros(partial.shape, f32)
     for k, (h, tile) in enumerate(order):
 
         @pl.when(k < places)
@@ -244,27 +262,61 @@
                         sums = product_sums(sums, [fields[k, a, rows, lanes] for a in range(3)], pair[half])
                 return sums
 
-            for i, value in enumerate(packed_sums(sums_of, cells // LANES)):
+            for i, value in enumerate(packed_sums(sums_of, depth)):
                 out[h, i] = value
 
-
-def call_heavy_moments(helper_tile, base_fields, base_noise):
+    @pl.loop(0, pieces)
+    def _(r):
+        for copy in piece_loads(r):
+            copy.wait()
+
+        def at(x):
+            lanes = pl.ds(pl.multiple_of(x * LANES, LANES), LANES)
+            sums = [partial[i, x] for i in range(24)]
+            for group in range(2):
+                start = pl.multiple_of(r * each + group * 2 * SUB, 2 * SUB)
+                one, two = [
+                    noise_rows(lambda a, rows: near_noise[step, a, rows, lanes], start) for step in range(2)
+                ]
+                for half in range(2):
+                    q = [near[a, pl.ds(start + half * SUB, SUB), lanes] for a in range(3)]
+                    sums = later_sums(sums, q, one[half], two[half])
+            for i, value in enumerate(sums):
+                partial[i, x] = value
+
+        @pl.loop(0, depth // 4)
+        def _(x):
+            for i in range(4):
+                at(4 * x + i)
+
+    for i in range(24):
+        later[i] = packed_sums(lambda x: [partial[i, x]], depth)[0]
+
+
+def call_early_sums(helper_tile, base_fields, base_noise, extra_fields, extra_noise):
     slots = helper_tile.shape[1]
     count, cells = base_fields.shape[-2:]
+    depth = cells // LANES
     return pl.pallas_call(
-        heavy_moments,
-        out_shape=jax.ShapeDtypeStruct((slots, 16, cells // LANES, LANES), f32),
-        in_specs=[vmem, hbm, hbm],
-        out_specs=vmem,
+        early_sums,
+        out_shape=(
+            jax.ShapeDtypeStruct((slots, 16, depth, LANES), f32),
+            jax.ShapeDtypeStruct((24, depth, LANES), f32),
+        ),
+        in_specs=[vmem, hbm, hbm, hbm, hbm],
+        out_specs=(vmem, vmem),
         scratch_shapes=[
             pltpu.VMEM((HEAVY_MOST, 3, count, cells), f32),
             pltpu.VMEM((HEAVY_MOST, 3, count, cells), jnp.bfloat16),
-            pltpu.SemaphoreType.DMA((2, HEAVY_MOST)),
+            pltpu.VMEM(extra_fields.shape[2:], f32),
+            pltpu.VMEM(extra_noise.shape[2:], jnp.bfloat16),
+            pltpu.VMEM((24, depth, SUB, LANES), f32),
+            pltpu.SemaphoreType.DMA((2, HEAVY_MOST + extra_fields.shape[3] // (4 * SUB))),
         ],
         compiler_params=pltpu.CompilerParams(vmem_limit_bytes=SMALL),
         cost_estimate=small(8 << 20, 3 << 20),
-        name="heavy_moments",
-    )(helper_tile, *far_memory(base_fields, base_noise))
+        name="early_sums",
+    )(helper_tile, *far_memory(base_fields, base_noise, extra_fields, extra_noise))
 
 
 def outer_sums(sums, left, right):
@@ -802,8 +854,7 @@
     x_one = swap_within(x_one, "gx")
     y_one = swap_within(y_one, "gy")
     halos = (y_two, x_two, x_one, y_one)
-    moments = call_heavy_moments(helper_tile, base_fields, base_noise)
-    later = call_extra_moments(2, moments, extra_fields, extra_noise)
+    moments, later = call_early_sums(helper_tile, base_fields, base_noise, extra_fields, extra_noise)
     grad, keep, send = call_gradients(tiles, later, helper_tile, velocity, halos, wall_cells, moments)
     some = 3 * tiles // 8
     ordinary_fields = (base_fields, base_noise, grad)

time: 31.3 us -> 31.8 us (1.016)
  the two profiles are of different devices: /device:TPU:0 before, /device:TPU:1 now
where the time goes in v1:
time: 31.8 us; the launch traced here: 31.6 us
  Pallas kernels  16.4 us (52%)
  starting transfers between devices  14.1 us (44%)
  between operations  0.86 us (3%)
    ppermute x8, starting transfers between devices, swapped(): return lax.ppermute(block, 'gy', [(i, i ^ flip) for i in range(size)])  7.76 us
    pallas_call x3, Pallas kernels, call_ordinary(): pl.pallas_call(functools.partial(ordinary, first, direct, has_block, has_...  5.16 us
    pallas_call x1, Pallas kernels, call_early_sums(): pl.pallas_call(early_sums, out_shape=(jax.ShapeDtypeStruct((slots, 16, de...  4.5 us
    ppermute x2, starting transfers between devices, swap_within(): lax.ppermute(block, axis, [(i, i ^ 1) for i in range(lax.axis_size(axis))])  3.15 us
    ppermute x2, starting transfers between devices, swap_across(): lax.ppermute(block, ('gx', 'gy'), [(i, partner(*place)) for i, place in e...  3.15 us
    pallas_call x1, Pallas kernels, call_finish(): pl.pallas_call(functools.partial(finish, len(pieces)), out_shape=(jax.Sha...  1.95 us
    pallas_call x1, Pallas kernels, call_extra_moments(): pl.pallas_call(functools.partial(extra_moments, steps, 7), out_shape=jax....  1.59 us
    pallas_call x1, Pallas kernels, call_final(): pl.pallas_call(final, out_shape=(jax.ShapeDtypeStruct(new_base.shape, f32...  1.37 us
  transfers between devices with their start and end apart: 12, of which 1 were waited for; matrix products, arithmetic and copies ran while one was open for 0% of the time, Pallas kernels for 42%

profile of v1, /device:TPU:1, one launch (start us, length us, event | category | flops | bytes accessed | tf_op | source)
XLA Modules:
  0.0 31.6 jit_solution(3940520860105615428)
XLA Ops:
  0.6 0.9 %edges.1 = (s32[1,8]{1,0:T(1,128)S(1)}, f32[3,8,128]{2,1,0:T(8,128)S(1)}, f32[3,8,128]{2,1,0:T(8,128)S(1)}, f32[3,8,128]{2,1,0:T(8,128)S(1)}, f32[3,8,128]{2,1,0:T(8,128)S(1)}) custom-call(s32[1,8]{1,0:T(1,128)} %helper.1, f32[3,8,8,128]{3,2,1,0:T(8,128)} %velocity.3), custom_call_target="tpu_custom_call" | custom-call | flops 1024 | bytes 131072 | tf_op jit(solution)/shard_map/edges/pallas_call | solution.py:172
  1.6 2.7 %collective-permute-start = (f32[3,8,128]{2,1,0:T(8,128)S(1)}, f32[3,8,128]{2,1,0:T(8,128)S(1)}, u32[]{:S(2)}, u32[]{:S(2)}) collective-permute-start(f32[3,8,128]{2,1,0:T(8,128)S(1)} %get-tuple-element.34), channel_id=1, source_target_pairs={{0,8},{1,2},{2,1},{3,4},{4,3},{5,6},{6,5},{7,15},{8,0},{9,10},{10,... | collective-permute-start | bytes 36872 | tf_op jit(solution)/shard_map/ppermute | solution.py:201
  4.2 0.5 %collective-permute-start.1 = (f32[3,8,128]{2,1,0:T(8,128)S(1)}, f32[3,8,128]{2,1,0:T(8,128)S(1)}, u32[]{:S(2)}, u32[]{:S(2)}) collective-permute-start(f32[3,8,128]{2,1,0:T(8,128)S(1)} %get-tuple-element.35), channel_id=1, source_target_pairs={{0,1},{1,0},{2,3},{3,2},{4,5},{5,4},{6,7},{7,6},{8,16},{9,17},{10,... | collective-permute-start | bytes 36872 | tf_op jit(solution)/shard_map/ppermute | solution.py:201
  4.7 2.1 %collective-permute-start.2 = (f32[3,8,128]{2,1,0:T(8,128)S(1)}, f32[3,8,128]{2,1,0:T(8,128)S(1)}, u32[]{:S(2)}, u32[]{:S(2)}) collective-permute-start(f32[3,8,128]{2,1,0:T(8,128)S(1)} %get-tuple-element.36), channel_id=1, source_target_pairs={{0,8},{8,0},{16,24},{24,16},{1,9},{9,1},{17,25},{25,17},{2,10},{10... | collective-permute-start | bytes 36872 | tf_op jit(solution)/shard_map/ppermute | solution.py:184
  6.8 1.0 %collective-permute-start.3 = (f32[3,8,128]{2,1,0:T(8,128)S(1)}, f32[3,8,128]{2,1,0:T(8,128)S(1)}, u32[]{:S(2)}, u32[]{:S(2)}) collective-permute-start(f32[3,8,128]{2,1,0:T(8,128)S(1)} %get-tuple-element.37), channel_id=1, source_target_pairs={{0,1},{1,0},{2,3},{3,2},{4,5},{5,4},{6,7},{7,6},{8,9},{9,8},{10,11... | collective-permute-start | bytes 36872 | tf_op jit(solution)/shard_map/ppermute | solution.py:184
  7.9 4.5 %early_sums.1 = (f32[8,16,8,128]{3,2,1,0:T(8,128)S(1)}, f32[24,8,128]{2,1,0:T(8,128)S(1)}) custom-call(s32[1,8]{1,0:T(1,128)S(1)} %get-tuple-element.32.helper, f32[1,1,8,3,32,1024]{5,4,3,2,1,0:T(8,128)} %base.7, bf16[1,1,8,2,3,32,1024]{6,5,4,3,2,1,0:T(8,128)(2,1)} %noise.7, f32[1,1,3,224,1024]{4,3,2,1,0:T(8,128)} %refs_6_.1, ...), custom_call_target="tpu_custom_call" | custom-call | flops 8388608 | bytes 3145728 | tf_op jit(solution)/shard_map/early_sums/pallas_call | solution.py:300
  12.4 0.0 collective-permute-done.y_two
  12.4 0.0 collective-permute-done.2.x_one
  12.4 0.0 collective-permute-done.3.y_one
  12.4 0.8 %gradients.1 = (f32[576,128]{1,0:T(8,128)S(1)}, f32[4,12,8,128]{3,2,1,0:T(8,128)S(1)}, f32[4,12,8,128]{3,2,1,0:T(8,128)S(1)}) custom-call(f32[24,8,128]{2,1,0:T(8,128)S(1)} %get-tuple-element.33.before.later, s32[1,8]{1,0:T(1,128)S(1)} %get-tuple-element.32.helper, f32[3,8,8,128]{3,2,1,0:T(8,128)S(1)} %copy-done.4, ...), custom_call_target="tpu_custom_call" | custom-call | flops 4194304 | bytes 1048576 | tf_op jit(solution)/shard_map/gradients/pallas_call | solution.py:422
  13.2 0.1 collective-permute-start.4
  13.3 0.0 copy-start.2
  13.3 0.0 copy-start.3
  13.3 1.1 %ordinary_tiles.3 = (f32[3,3,32,1024]{3,2,1,0:T(8,128)S(1)}, f32[6,3,8,128]{3,2,1,0:T(8,128)S(1)}) custom-call(f32[4,12,8,128]{3,2,1,0:T(8,128)S(1)} %get-tuple-element.40.refs_0_, f32[1,1,8,3,32,1024]{5,4,3,2,1,0:T(8,128)S(1)} %copy-done, bf16[1,1,8,2,3,32,1024]{6,5,4,3,2,1,0:T(8,128)(2,1)S(1)} %copy-done.1, f32[576,128]{1,0:T(8,128)S(1)} %get-tuple-element.39.refs_3_.grad), custom_call_target="tpu_custom_call" | custom-call | flops 8388608 | bytes 3145728 | tf_op jit(solution)/shard_map/ordinary_tiles/pallas_call | solution.py:635
  14.5 0.2 collective-permute-done.4.received
  14.8 0.1 collective-permute-start.5
  14.8 0.9 %collective-permute-start.6 = (f32[12,8,128]{2,1,0:T(8,128)S(1)}, f32[12,8,128]{2,1,0:T(8,128)S(1)}, u32[]{:S(2)}, u32[]{:S(2)}) collective-permute-start(f32[12,8,128]{2,1,0:T(8,128)S(1)} %get-tuple-element.43.before), channel_id=1, source_target_pairs={{0,2},{1,3},{2,0},{3,1},{4,6},{5,7},{6,4},{7,5},{8,10},{9,11},{10,... | collective-permute-start | bytes 147464 | tf_op jit(solution)/shard_map/ppermute | solution.py:435
  15.8 1.7 %collective-permute-start.7 = (f32[12,8,128]{2,1,0:T(8,128)S(1)}, f32[12,8,128]{2,1,0:T(8,128)S(1)}, u32[]{:S(2)}, u32[]{:S(2)}) collective-permute-start(f32[12,8,128]{2,1,0:T(8,128)S(1)} %get-tuple-element.48), channel_id=1, source_target_pairs={{0,4},{1,5},{2,6},{3,7},{4,0},{5,1},{6,2},{7,3},{8,12},{9,13},{10,... | collective-permute-start | bytes 147464 | tf_op jit(solution)/shard_map/ppermute | solution.py:435
  17.5 1.6 %extra_moments.1.refs_0_.moments = f32[21,8,128]{2,1,0:T(8,128)S(1)} custom-call(f32[12,8,128]{2,1,0:T(8,128)S(1)} %get-tuple-element.43.before, f32[1,1,3,224,1024]{4,3,2,1,0:T(8,128)S(1)} %copy-done.2, bf16[1,1,2,3,224,1024]{5,4,3,2,1,0:T(8,128)(2,1)S(1)} %copy-done.3), custom_call_target="tpu_custom_call" | custom-call | flops 8388608 | bytes 5242880 | tf_op jit(solution)/shard_map/extra_moments/pallas_call | solution.py:357
  19.1 1.0 %ordinary_tiles.4 = (f32[1,1,8,3,32,1024]{5,4,3,2,1,0:T(8,128)}, f32[2,3,32,1024]{3,2,1,0:T(8,128)S(1)}, f32[6,2,8,128]{3,2,1,0:T(8,128)S(1)}) custom-call(f32[21,8,128]{2,1,0:T(8,128)S(1)} %extra_moments.1.refs_0_.moments, f32[1,1,8,3,32,1024]{5,4,3,2,1,0:T(8,128)S(1)} %copy-done, bf16[1,1,8,2,3,32,1024]{6,5,4,3,2,1,0:T(8,128)(2,1)S(1)} %copy-done.1, ...), custom_call_target="tpu_custom_call" | custom-call | flops 8388608 | bytes 3145728 | tf_op jit(solution)/shard_map/ordinary_tiles/pallas_call | solution.py:635
  20.1 0.0 collective-permute-done.6.refs_2_
  20.1 0.0 collective-permute-done.7.refs_3_
  20.1 0.1 answering.1
  20.3 0.1 collective-permute-start.10
  20.4 1.7 %collective-permute-start.8 = (f32[8,8,128]{2,1,0:T(8,128)S(1)}, f32[8,8,128]{2,1,0:T(8,128)S(1)}, u32[]{:S(2)}, u32[]{:S(2)}) collective-permute-start(f32[8,8,128]{2,1,0:T(8,128)S(1)} %get-tuple-element.49.refs_0_), channel_id=1, source_target_pairs={{0,2},{1,3},{2,0},{3,1},{4,6},{5,7},{6,4},{7,5},{8,10},{9,11},{10,... | collective-permute-start | bytes 98312 | tf_op jit(solution)/shard_map/ppermute | solution.py:435
  22.1 0.9 %collective-permute-start.9 = (f32[8,8,128]{2,1,0:T(8,128)S(1)}, f32[8,8,128]{2,1,0:T(8,128)S(1)}, u32[]{:S(2)}, u32[]{:S(2)}) collective-permute-start(f32[8,8,128]{2,1,0:T(8,128)S(1)} %get-tuple-element.49.refs_0_), channel_id=1, source_target_pairs={{0,4},{1,5},{2,6},{3,7},{4,0},{5,1},{6,2},{7,3},{8,12},{9,13},{10,... | collective-permute-start | bytes 98312 | tf_op jit(solution)/shard_map/ppermute | solution.py:435
  23.0 3.0 %ordinary_tiles.5 = (f32[1,1,8,3,32,1024]{5,4,3,2,1,0:T(8,128)}, f32[1,1,3,224,1024]{4,3,2,1,0:T(8,128)}, f32[2,3,32,1024]{3,2,1,0:T(8,128)S(1)}, f32[6,3,8,128]{3,2,1,0:T(8,128)S(1)}) custom-call(f32[8,8,128]{2,1,0:T(8,128)S(1)} %get-tuple-element.49.refs_0_, f32[1,1,8,3,32,1024]{5,4,3,2,1,0:T(8,128)S(1)} %copy-done, ...), custom_call_target="tpu_custom_call", output_to_operand_aliasing={{0}: (5, {})} | custom-call | flops 8388608 | bytes 3145728 | tf_op jit(solution)/shard_map/ordinary_tiles/pallas_call | solution.py:635
  26.0 0.0 collective-permute-done.8.refs_1_
  26.0 0.0 collective-permute-done.9.refs_2_
  26.0 2.3 %collective-permute-start.11 = (f32[4,8,8,128]{3,2,1,0:T(8,128)S(1)}, f32[4,8,8,128]{3,2,1,0:T(8,128)S(1)}, u32[]{:S(2)}, u32[]{:S(2)}) collective-permute-start(f32[4,8,8,128]{3,2,1,0:T(8,128)S(1)} %join.1.near), channel_id=1, source_target_pairs={{0,1},{1,0},{2,3},{3,2},{4,5},{5,4},{6,7},{7,6},{8,9},{9,8},{10,11... | collective-permute-start | bytes 393224 | tf_op jit(solution)/shard_map/ppermute | solution.py:435
  28.3 2.0 %finish.1 = (f32[1,1,8,3,32,1024]{5,4,3,2,1,0:T(8,128)}, f32[6,8,8,128]{3,2,1,0:T(8,128)S(1)}) custom-call(s32[1,8]{1,0:T(1,128)S(1)} %get-tuple-element.32.helper, f32[1,1,8,3,32,1024]{5,4,3,2,1,0:T(8,128)S(1)} %copy-done, bf16[1,1,8,2,3,32,1024]{6,5,4,3,2,1,0:T(8,128)(2,1)S(1)} %copy-done.1, ...), custom_call_target="tpu_custom_call", output_to_operand_aliasing={{0}: (9, {})} | custom-call | flops 1024 | bytes 1048576 | tf_op jit(solution)/shard_map/finish/pallas_call | solution.py:792
  30.3 1.4 %heavy_tiles.1 = (f32[1,1,8,3,32,1024]{5,4,3,2,1,0:T(8,128)}, f32[1,1,6,8,1024]{4,3,2,1,0:T(8,128)}) custom-call(s32[1,8]{1,0:T(1,128)S(1)} %get-tuple-element.32.helper, f32[1,1,8,3,32,1024]{5,4,3,2,1,0:T(8,128)S(1)} %copy-done, bf16[1,1,8,2,3,32,1024]{6,5,4,3,2,1,0:T(8,128)(2,1)S(1)} %copy-done.1, ...), custom_call_target="tpu_custom_call", output_to_operand_aliasing={{0}: (6, {})} | custom-call | flops 8388608 | bytes 4194304 | tf_op jit(solution)/shard_map/heavy_tiles/pallas_call | solution.py:828
  (16 shorter events, 0.1 us)
Async XLA Ops:
  1.6 10.8 %collective-permute-start = (f32[3,8,128]{2,1,0:T(8,128)S(1)}, f32[3,8,128]{2,1,0:T(8,128)S(1)}, u32[]{:S(2)}, u32[]{:S(2)}) collective-permute-start(f32[3,8,128]{2,1,0:T(8,128)S(1)} %get-tuple-element.34), channel_id=1, source_target_pairs={{0,8},{1,2},{2,1},{3,4},{4,3},{5,6},{6,5},{7,15},{8,0},{9,10},{10,... | collective-permute-start | bytes 36872 | tf_op jit(solution)/shard_map/ppermute | solution.py:201
  4.2 8.2 %collective-permute-start.1 = (f32[3,8,128]{2,1,0:T(8,128)S(1)}, f32[3,8,128]{2,1,0:T(8,128)S(1)}, u32[]{:S(2)}, u32[]{:S(2)}) collective-permute-start(f32[3,8,128]{2,1,0:T(8,128)S(1)} %get-tuple-element.35), channel_id=1, source_target_pairs={{0,1},{1,0},{2,3},{3,2},{4,5},{5,4},{6,7},{7,6},{8,16},{9,17},{10,... | collective-permute-start | bytes 36872 | tf_op jit(solution)/shard_map/ppermute | solution.py:201
  4.7 7.7 %collective-permute-start.2 = (f32[3,8,128]{2,1,0:T(8,128)S(1)}, f32[3,8,128]{2,1,0:T(8,128)S(1)}, u32[]{:S(2)}, u32[]{:S(2)}) collective-permute-start(f32[3,8,128]{2,1,0:T(8,128)S(1)} %get-tuple-element.36), channel_id=1, source_target_pairs={{0,8},{8,0},{16,24},{24,16},{1,9},{9,1},{17,25},{25,17},{2,10},{10... | collective-permute-start | bytes 36872 | tf_op jit(solution)/shard_map/ppermute | solution.py:184
  6.8 5.6 %collective-permute-start.3 = (f32[3,8,128]{2,1,0:T(8,128)S(1)}, f32[3,8,128]{2,1,0:T(8,128)S(1)}, u32[]{:S(2)}, u32[]{:S(2)}) collective-permute-start(f32[3,8,128]{2,1,0:T(8,128)S(1)} %get-tuple-element.37), channel_id=1, source_target_pairs={{0,1},{1,0},{2,3},{3,2},{4,5},{5,4},{6,7},{7,6},{8,9},{9,8},{10,11... | collective-permute-start | bytes 36872 | tf_op jit(solution)/shard_map/ppermute | solution.py:184
  7.9 4.6 %copy-start.4 = (f32[3,8,8,128]{3,2,1,0:T(8,128)S(1)}, f32[3,8,8,128]{3,2,1,0:T(8,128)}, u32[]{:S(2)}) copy-start(f32[3,8,8,128]{3,2,1,0:T(8,128)} %velocity.3) | copy-start | bytes 294916
  7.9 4.6 %copy-start.5 = (s32[8,8,128]{2,1,0:T(8,128)S(1)}, s32[8,8,128]{2,1,0:T(8,128)}, u32[]{:S(2)}) copy-start(s32[8,8,128]{2,1,0:T(8,128)} %wall.1) | copy-start | bytes 98308
  7.9 5.4 %copy-start = (f32[1,1,8,3,32,1024]{5,4,3,2,1,0:T(8,128)S(1)}, f32[1,1,8,3,32,1024]{5,4,3,2,1,0:T(8,128)}, u32[]{:S(2)}) copy-start(f32[1,1,8,3,32,1024]{5,4,3,2,1,0:T(8,128)} %base.7) | copy-start | bytes 9437188
  7.9 5.4 %copy-start.1 = (bf16[1,1,8,2,3,32,1024]{6,5,4,3,2,1,0:T(8,128)(2,1)S(1)}, bf16[1,1,8,2,3,32,1024]{6,5,4,3,2,1,0:T(8,128)(2,1)}, u32[]{:S(2)}) copy-start(bf16[1,1,8,2,3,32,1024]{6,5,4,3,2,1,0:T(8,128)(2,1)} %noise.7) | copy-start | bytes 9437188
  13.2 1.5 %collective-permute-start.4 = (f32[4,12,8,128]{3,2,1,0:T(8,128)S(1)}, f32[4,12,8,128]{3,2,1,0:T(8,128)S(1)}, u32[]{:S(2)}, u32[]{:S(2)}) collective-permute-start(f32[4,12,8,128]{3,2,1,0:T(8,128)S(1)} %get-tuple-element.40.refs_0_), channel_id=1, source_target_pairs={{0,1},{1,0},{2,3},{3,2},{4,5},{5,4},{6,7},{7,6},{8,9},{9,8},{10,11... | collective-permute-start | bytes 589832 | tf_op jit(solution)/shard_map/ppermute | solution.py:435
  13.3 4.2 %copy-start.2 = (f32[1,1,3,224,1024]{4,3,2,1,0:T(8,128)S(1)}, f32[1,1,3,224,1024]{4,3,2,1,0:T(8,128)}, u32[]{:S(2)}) copy-start(f32[1,1,3,224,1024]{4,3,2,1,0:T(8,128)} %refs_6_.1) | copy-start | bytes 8257540
  13.3 4.1 %copy-start.3 = (bf16[1,1,2,3,224,1024]{5,4,3,2,1,0:T(8,128)(2,1)S(1)}, bf16[1,1,2,3,224,1024]{5,4,3,2,1,0:T(8,128)(2,1)}, u32[]{:S(2)}) copy-start(bf16[1,1,2,3,224,1024]{5,4,3,2,1,0:T(8,128)(2,1)} %refs_7_.1) | copy-start | bytes 8257540
  14.8 5.4 %collective-permute-start.5 = (f32[12,8,128]{2,1,0:T(8,128)S(1)}, f32[12,8,128]{2,1,0:T(8,128)S(1)}, u32[]{:S(2)}, u32[]{:S(2)}) collective-permute-start(f32[12,8,128]{2,1,0:T(8,128)S(1)} %get-tuple-element.47), channel_id=1, source_target_pairs={{0,6},{1,7},{2,4},{3,5},{4,2},{5,3},{6,0},{7,1},{8,14},{9,15},{10,... | collective-permute-start | bytes 147464 | tf_op jit(solution)/shard_map/ppermute | solution.py:435
  14.8 5.3 %collective-permute-start.6 = (f32[12,8,128]{2,1,0:T(8,128)S(1)}, f32[12,8,128]{2,1,0:T(8,128)S(1)}, u32[]{:S(2)}, u32[]{:S(2)}) collective-permute-start(f32[12,8,128]{2,1,0:T(8,128)S(1)} %get-tuple-element.43.before), channel_id=1, source_target_pairs={{0,2},{1,3},{2,0},{3,1},{4,6},{5,7},{6,4},{7,5},{8,10},{9,11},{10,... | collective-permute-start | bytes 147464 | tf_op jit(solution)/shard_map/ppermute | solution.py:435
  15.8 4.4 %collective-permute-start.7 = (f32[12,8,128]{2,1,0:T(8,128)S(1)}, f32[12,8,128]{2,1,0:T(8,128)S(1)}, u32[]{:S(2)}, u32[]{:S(2)}) collective-permute-start(f32[12,8,128]{2,1,0:T(8,128)S(1)} %get-tuple-element.48), channel_id=1, source_target_pairs={{0,4},{1,5},{2,6},{3,7},{4,0},{5,1},{6,2},{7,3},{8,12},{9,13},{10,... | collective-permute-start | bytes 147464 | tf_op jit(solution)/shard_map/ppermute | solution.py:435
  20.3 5.7 %collective-permute-start.10 = (f32[8,8,128]{2,1,0:T(8,128)S(1)}, f32[8,8,128]{2,1,0:T(8,128)S(1)}, u32[]{:S(2)}, u32[]{:S(2)}) collective-permute-start(f32[8,8,128]{2,1,0:T(8,128)S(1)} %get-tuple-element.49.refs_0_), channel_id=1, source_target_pairs={{0,6},{1,7},{2,4},{3,5},{4,2},{5,3},{6,0},{7,1},{8,14},{9,15},{10,... | collective-permute-start | bytes 98312 | tf_op jit(solution)/shard_map/ppermute | solution.py:435
  20.4 5.6 %collective-permute-start.8 = (f32[8,8,128]{2,1,0:T(8,128)S(1)}, f32[8,8,128]{2,1,0:T(8,128)S(1)}, u32[]{:S(2)}, u32[]{:S(2)}) collective-permute-start(f32[8,8,128]{2,1,0:T(8,128)S(1)} %get-tuple-element.49.refs_0_), channel_id=1, source_target_pairs={{0,2},{1,3},{2,0},{3,1},{4,6},{5,7},{6,4},{7,5},{8,10},{9,11},{10,... | collective-permute-start | bytes 98312 | tf_op jit(solution)/shard_map/ppermute | solution.py:435
  22.1 3.9 %collective-permute-start.9 = (f32[8,8,128]{2,1,0:T(8,128)S(1)}, f32[8,8,128]{2,1,0:T(8,128)S(1)}, u32[]{:S(2)}, u32[]{:S(2)}) collective-permute-start(f32[8,8,128]{2,1,0:T(8,128)S(1)} %get-tuple-element.49.refs_0_), channel_id=1, source_target_pairs={{0,4},{1,5},{2,6},{3,7},{4,0},{5,1},{6,2},{7,3},{8,12},{9,13},{10,... | collective-permute-start | bytes 98312 | tf_op jit(solution)/shard_map/ppermute | solution.py:435
  26.0 4.2 %collective-permute-start.11 = (f32[4,8,8,128]{3,2,1,0:T(8,128)S(1)}, f32[4,8,8,128]{3,2,1,0:T(8,128)S(1)}, u32[]{:S(2)}, u32[]{:S(2)}) collective-permute-start(f32[4,8,8,128]{3,2,1,0:T(8,128)S(1)} %join.1.near), channel_id=1, source_target_pairs={{0,1},{1,0},{2,3},{3,2},{4,5},{5,4},{6,7},{7,6},{8,9},{9,8},{10,11... | collective-permute-start | bytes 393224 | tf_op jit(solution)/shard_map/ppermute | solution.py:435
